TPU v7x, 32 devices: a whole 2x2x4 slice. The times are simulated.
32 devices in a mesh: groups: 2 (over x), tile: 16 (over z, y, core).
Axes of the slice: x: 2, y: 2, z: 4, core: 2. Of those that a mesh axis runs over, the one named last changes fastest.
Arguments:
- model_field: float32 [16, 524288], P(None, ('groups', 'tile')), parts along dimension 1, may hold values from -6 to 6
- direction: float32 [16, 524288], P(None, ('groups', 'tile')), parts along dimension 1, may hold values from -100 to 100
- old_grad: float32 [16, 524288], P(None, ('groups', 'tile')), parts along dimension 1, may hold values from -100 to 100
- residual: float32 [16, 65536], P(None, ('groups', 'tile')), parts along dimension 1, may hold values from -6 to 6
- block_pairs: int32 [256, 8], P(('groups', 'tile')), parts along dimension 0, may hold values from 0 to 159, as said below
- depth_band: int32 [524288], P(('groups', 'tile')), parts along dimension 0, may hold values from 0 to 15
- station_offsets: float32 [2, 65536], P(None, ('groups', 'tile')), parts along dimension 1, may hold values from -1.25 to 2.25, as said below
Outputs:
- new_model: float32 [16, 524288], P(None, ('groups', 'tile')), parts along dimension 1
- new_residual: float32 [16, 65536], P(None, ('groups', 'tile')), parts along dimension 1
- new_direction: float32 [16, 524288], P(None, ('groups', 'tile')), parts along dimension 1
There are 2 independent parts, one for each index of `groups`. A program takes and returns all parts, laid end to end along the dimension named above; each array names one. Nothing has to cross between parts.
Inputs may be any that keep to these rules, and one draw needn't show every extreme that they name: `block_pairs`: each row lists 8 different codes. `station_offsets`: row 1 (along) lies between 0 and 1.
All inputs are finite; a program needn't handle non-finite values.
Results may differ from a plain program's by a relative error of at most 0.0003.
Values sent between devices are 32-bit elements; how exact they have to be, the bound alone decides.
A program may use at most 128 MiB of HBM per device.

v0:
```python
import functools
import math

import jax
import jax.numpy as jnp
from jax import lax
from jax.experimental import pallas as pl
from jax.experimental.pallas import tpu as pltpu
from jax.sharding import PartitionSpec as P

CBLOCK = 512
SBLOCK = 256
REACH = 2
BANDS = 16
COL_SIDE = 32
DEPTH_RANGE = 2.0
DEPTH_SHIFT = 0.25
DAMPING = 1.0
GUARD = 1e-06

SPAN = 2 * REACH + 1
HOPS = tuple(r for r in range(-REACH, REACH + 1) if r != 0)
UNROLL = 8
MESH = pl.DeviceIdType.MESH
F32 = jnp.float32
BF16 = jnp.bfloat16
VMEM_LIMIT = 48 * 1024 * 1024


def exists(me, r, n):
    return jnp.logical_and(me + r >= 0, me + r < n)


def split(x):
    high = x.astype(BF16)
    return high, (x - high.astype(F32)).astype(BF16)


def lane_sums(x):
    total = jnp.sum(x, axis=0, keepdims=True)
    out = total[:, 0:128]
    for k in range(1, x.shape[1] // 128):
        out = out + total[:, k * 128 : (k + 1) * 128]
    return out


def exchange_kernel(
    n, scale, blocks, dirn, pairs, band, offs,
    st_o, codes_o, v_o, f_o, z_o, norm_o, send_sem, recv_sem,
):
    me = lax.axis_index("tile")
    rows = pairs.shape[0]
    barrier = pltpu.get_barrier_semaphore()
    for r in HOPS:
        @pl.when(exists(me, r, n))
        def _():
            pl.semaphore_signal(barrier, inc=1, device_id={"tile": me + r}, device_id_type=MESH)

    own = REACH * rows
    for k in range(rows):
        st_o[own + k] = offs[:, k * SBLOCK : (k + 1) * SBLOCK]
    codes_o[REACH] = pairs[...]
    for r in HOPS:
        @pl.when(jnp.logical_not(exists(me, r, n)))
        def _():
            t = r + REACH
            st_o[t * rows : (t + 1) * rows] = jnp.zeros((rows,) + st_o.shape[1:], F32)
            codes_o[t] = jnp.full(codes_o.shape[1:], -1, jnp.int32)

    peers = sum(exists(me, r, n).astype(jnp.int32) for r in HOPS)
    pl.semaphore_wait(barrier, peers)

    def copies(q, r):
        t = REACH - r
        made = []
        for which, (src, dst) in enumerate((
            (codes_o.at[REACH], codes_o.at[t]),
            (st_o.at[pl.ds(own, rows)], st_o.at[pl.ds(t * rows, rows)]),
        )):
            made.append(pltpu.make_async_remote_copy(
                src_ref=src, dst_ref=dst, send_sem=send_sem.at[which, q],
                recv_sem=recv_sem.at[which, q], device_id={"tile": me + r}, device_id_type=MESH,
            ))
        return made

    for q, r in enumerate(HOPS):
        @pl.when(exists(me, r, n))
        def _():
            for one in copies(q, r):
                one.start()

    depth = (band[...].astype(F32) + 0.5) * (DEPTH_RANGE / BANDS)
    shifted = depth + DEPTH_SHIFT
    f_o[...] = scale * depth * (shifted * jnp.sqrt(shifted))
    z_o[...] = (depth * depth).T

    def block(b, total):
        for q in range(CBLOCK // 128):
            lanes = pl.ds(pl.multiple_of(b * CBLOCK + q * 128, 128), 128)
            values = dirn[:, lanes]
            high, low = split(f_o[pl.ds(b * (CBLOCK // 128) + q, 1), :] * values)
            v_o[b, 0:16, q * 128 : (q + 1) * 128] = high
            v_o[b, 16:32, q * 128 : (q + 1) * 128] = low
            total = total + values * values
        return total

    total = lax.fori_loop(0, blocks, block, jnp.zeros((dirn.shape[0], 128), F32))
    norm_o[...] = jnp.concatenate(
        [jnp.zeros((1, 128), F32), lane_sums(total), jnp.zeros((6, 128), F32)], axis=0
    )

    for q, r in enumerate(HOPS):
        @pl.when(exists(me, r, n))
        def _():
            for one in copies(q, r):
                one.wait_send()

        @pl.when(exists(me, -r, n))
        def _():
            for one in copies(q, r):
                one.wait_recv()


def kernel_halves(entry, st, z):
    j = lax.shift_right_logical(entry, 5)
    b = lax.bitwise_and(entry, 31)
    at = jnp.minimum(j, st.shape[0] - 1)
    rows = st.shape[0] // SPAN
    moved = (at // rows - REACH).astype(F32)
    parity = lax.bitwise_and(b, 1).astype(F32)
    place = st[at]
    sx = place[0:1, :] + moved
    sy = place[1:2, :] - 0.5 * parity
    column = (lax.broadcasted_iota(jnp.int32, (COL_SIDE, SBLOCK), 0).astype(F32) + 0.5) / COL_SIDE
    across = sx - column
    across = across * across
    which = jnp.full((COL_SIDE, 128), b * (CBLOCK // 128), jnp.int32)
    halves = []
    for h in range(2):
        highs, lows = [], []
        for a in range(h * 8, h * 8 + 8):
            along = sy - (a + 0.5) / COL_SIDE
            along = along * along
            low_row = a % 4 * COL_SIDE
            picked = jnp.take_along_axis(z[low_row : low_row + COL_SIDE, :], which + a // 4, axis=1)
            picked = jnp.concatenate([picked, picked], axis=1)
            inverse = lax.rsqrt(across + (along + picked))
            high, low = split(inverse * inverse * inverse)
            highs.append(high)
            lows.append(low)
        halves.append((jnp.concatenate(highs, axis=0), jnp.concatenate(lows, axis=0)))
    return j, b, halves


def forward_kernel(codes, st, z, v, img, pair_list, count):
    rows = codes.shape[1]
    img[...] = jnp.zeros(img.shape, F32)
    filled = jnp.int32(0)
    for t in range(SPAN):
        def pick(row, filled):
            for p in range(codes.shape[2]):
                code = codes[t, row, p]
                pair_list[filled] = (t * rows + row) * 32 + lax.bitwise_and(code, 31)
                hit = lax.shift_right_arithmetic(code, 5) == SPAN - 1 - t
                filled = filled + hit.astype(jnp.int32)
            return filled
        filled = lax.fori_loop(0, rows, pick, filled)
    for u in range(UNROLL):
        pair_list[filled + u] = SPAN * rows * 32
    steps = (filled + (UNROLL - 1)) // UNROLL
    count[0] = steps

    def step(i, carry):
        for u in range(UNROLL):
            j, b, halves = kernel_halves(pair_list[i * UNROLL + u], st, z)
            out = jnp.zeros((32, SBLOCK), F32)
            for h in range(2):
                values = v[b, :, h * 256 : (h + 1) * 256]
                for part in halves[h]:
                    out = out + jnp.dot(values, part, preferred_element_type=F32)
            img[j] += out[0:16] + out[16:32]
        return carry

    lax.fori_loop(0, steps, step, 0)


def all_sum(n, me, mine, landing, send_sem, recv_sem, start, finish):
    def made(k):
        return pltpu.make_async_remote_copy(
            src_ref=mine, dst_ref=landing.at[k], send_sem=send_sem.at[k], recv_sem=recv_sem.at[k],
            device_id={"tile": lax.rem(me + k, n)}, device_id_type=MESH,
        )
    if start:
        def go(k, c):
            made(k).start()
            return c
        lax.fori_loop(1, n, go, 0)
    if finish:
        def done(k, c):
            made(k).wait()
            return c
        lax.fori_loop(1, n, done, 0)


def greet_all(n, me):
    barrier = pltpu.get_barrier_semaphore()

    def greet(k, c):
        pl.semaphore_signal(
            barrier, inc=1, device_id={"tile": lax.rem(me + k, n)}, device_id_type=MESH
        )
        return c
    lax.fori_loop(1, n, greet, 0)
    pl.semaphore_wait(barrier, n - 1)


def image_kernel(
    n, rows, img, res, norm, old, newres_o, scal_o,
    transit, joined, part_rx, norm_tx, norm_rx, send_sem, recv_sem, nsend_sem, nrecv_sem,
):
    me = lax.axis_index("tile")
    greet_all(n, me)
    s = 1 - 2 * lax.rem(me, 2)
    outward = exists(me, -2 * s, n)
    inward = exists(me, 2 * s, n)

    def slab(ref, r):
        return ref.at[pl.ds((REACH + r) * rows, rows)]

    def copy(number, src, dst, to):
        return pltpu.make_async_remote_copy(
            src_ref=src, dst_ref=dst, send_sem=send_sem.at[number],
            recv_sem=recv_sem.at[number], device_id={"tile": to}, device_id_type=MESH,
        )

    to_join = copy(0, slab(img, 2 * s), transit, me + s)
    to_sibling = copy(1, slab(img, s), part_rx.at[0], me + s)
    to_far = copy(2, slab(img, -2 * s), part_rx.at[1], me - 2 * s)
    to_near = copy(3, joined, part_rx.at[2], me - s)
    own = slab(newres_o, 0)
    give_near = copy(4, own, slab(newres_o, s), me - s)
    give_far = copy(5, own, slab(newres_o, -2 * s), me + 2 * s)
    give_sibling = copy(6, own, slab(newres_o, -s), me + s)
    pass_on = copy(7, slab(newres_o, -s), slab(newres_o, -2 * s), me + s)

    @pl.when(inward)
    def _():
        to_join.start()

    @pl.when(outward)
    def _():
        to_far.start()
    to_sibling.start()

    def squares(k, total):
        values = old[:, pl.ds(pl.multiple_of(k * 512, 512), 512)]
        return total + values * values

    before = lax.fori_loop(0, old.shape[1] // 512, squares, jnp.zeros((old.shape[0], 512), F32))
    norm_tx[...] = norm[...]
    norm_tx[0:1, :] = lane_sums(before)

    @pl.when(outward)
    def _():
        to_join.wait_recv()
        joined[...] = transit[...] + img[pl.ds((REACH - s) * rows, rows)]
        to_near.start()

    to_sibling.wait_recv()
    here = REACH * rows
    newres_o[here : here + rows] = img[here : here + rows] + part_rx[0]

    @pl.when(inward)
    def _():
        to_far.wait_recv()
        newres_o[here : here + rows] += part_rx[1]

    @pl.when(outward)
    def _():
        to_near.wait_recv()
        newres_o[here : here + rows] += part_rx[2]

    image = newres_o[here : here + rows]
    norm_tx[2:3, :] = lane_sums(jnp.sum(image * image, axis=0))
    all_sum(n, me, norm_tx, norm_rx, nsend_sem, nrecv_sem, True, True)
    norm_rx[0] = norm_tx[...]
    totals = jnp.sum(jnp.sum(norm_rx[...], axis=0), axis=1, keepdims=True)
    gamma_old = totals[0:1]
    length = gamma_old / (totals[2:3] + DAMPING * totals[1:2] + GUARD)
    scal_o[...] = jnp.concatenate(
        [jnp.broadcast_to(length, (4, 128)), jnp.broadcast_to(gamma_old, (4, 128))], axis=0
    )
    for k in range(rows):
        newres_o[here + k] = res[:, k * SBLOCK : (k + 1) * SBLOCK] - length * newres_o[here + k]

    @pl.when(outward)
    def _():
        give_near.start()

    @pl.when(inward)
    def _():
        give_far.start()
    give_sibling.start()

    @pl.when(outward)
    def _():
        give_near.wait_recv()
        pass_on.start()
        to_far.wait_send()
        to_near.wait_send()
        give_far.wait_recv()
        give_near.wait_send()
        pass_on.wait_send()

    @pl.when(inward)
    def _():
        to_join.wait_send()
        give_far.wait_send()
        pass_on.wait_recv()
    to_sibling.wait_send()
    give_sibling.wait()


def adjoint_kernel(
    pair_list, count, st, z, f, newres, scal, model, dirn,
    model_hbm, grad_o, gamma_o, res_o, acc, parts, model_o, out_sem,
):
    slots = newres.shape[0]
    rows = slots // SPAN
    for k in range(rows):
        res_o[:, k * SBLOCK : (k + 1) * SBLOCK] = newres[REACH * rows + k]

    length = scal[0:1, 0:1]

    def update(b, c):
        lanes = pl.ds(pl.multiple_of(b * CBLOCK, CBLOCK), CBLOCK)
        model_o[:, lanes] = model[:, lanes] + length * dirn[:, lanes]
        return c
    lax.fori_loop(0, acc.shape[0], update, 0)
    leave = pltpu.make_async_copy(model_o, model_hbm, out_sem)
    leave.start()

    def cut(k, c):
        high, low = split(newres[k])
        parts[k, 0:16, :] = high
        parts[k, 16:32, :] = low
        return c
    lax.fori_loop(0, slots, cut, 0)
    parts[slots] = jnp.zeros((32, SBLOCK), BF16)
    acc[...] = jnp.zeros(acc.shape, F32)

    def step(i, carry):
        for u in range(UNROLL):
            j, b, halves = kernel_halves(pair_list[i * UNROLL + u], st, z)
            values = parts[j]
            for h in range(2):
                out = jnp.zeros((32, 256), F32)
                for part in halves[h]:
                    out = out + lax.dot_general(
                        values, part, (((1,), (1,)), ((), ())), preferred_element_type=F32
                    )
                acc[b, :, h * 256 : (h + 1) * 256] += out[0:16] + out[16:32]
        return carry

    lax.fori_loop(0, count[0], step, 0)

    def finish(b, total):
        lanes = pl.ds(pl.multiple_of(b * CBLOCK, CBLOCK), CBLOCK)
        new_model = model_o[:, lanes]
        factor = jnp.concatenate(
            [f[pl.ds(b * (CBLOCK // 128) + q, 1), :] for q in range(CBLOCK // 128)], axis=1
        )
        gradient = factor * acc[b] - DAMPING * new_model
        grad_o[:, lanes] = gradient
        return total + gradient * gradient

    total = lax.fori_loop(0, acc.shape[0], finish, jnp.zeros((model.shape[0], CBLOCK), F32))
    gamma_o[...] = jnp.concatenate([lane_sums(total), jnp.zeros((7, 128), F32)], axis=0)
    leave.wait()


def gamma_kernel(n, gamma, scal, ratio_o, landing, send_sem, recv_sem):
    me = lax.axis_index("tile")
    greet_all(n, me)
    all_sum(n, me, gamma, landing, send_sem, recv_sem, True, True)
    landing[0] = gamma[...]
    total = jnp.sum(jnp.sum(landing[...], axis=0), axis=1, keepdims=True)[0:1]
    ratio_o[...] = total / (scal[4:5, 0:1] + GUARD)


def shards(model_field, direction, old_grad, residual, block_pairs, depth_band, station_offsets):
    n = lax.axis_size("tile")
    epochs, cells = model_field.shape
    stations = residual.shape[1]
    rows = block_pairs.shape[0]
    pairs = block_pairs.shape[1]
    blocks = cells // CBLOCK
    scale = 2.0 / math.sqrt(cells)
    vmem = pl.BlockSpec(memory_space=pltpu.VMEM)
    smem = pl.BlockSpec(memory_space=pltpu.SMEM)
    shape = jax.ShapeDtypeStruct
    slots = SPAN * rows
    dma = pltpu.SemaphoreType.DMA

    def params(number=None):
        if number is None:
            return pltpu.CompilerParams(vmem_limit_bytes=VMEM_LIMIT)
        return pltpu.CompilerParams(
            vmem_limit_bytes=VMEM_LIMIT, collective_id=number, has_side_effects=True
        )

    st, codes, v, f, z, norm = pl.pallas_call(
        functools.partial(exchange_kernel, n, scale, blocks),
        out_shape=(
            shape((slots, 2, SBLOCK), F32),
            shape((SPAN, rows, pairs), jnp.int32),
            shape((blocks, 2 * epochs, CBLOCK), BF16),
            shape((cells // 128, 128), F32),
            shape((128, cells // 128), F32),
            shape((8, 128), F32),
        ),
        in_specs=[vmem] * 4,
        out_specs=(vmem,) * 6,
        scratch_shapes=[
            dma((2, len(HOPS))),
            dma((2, len(HOPS))),
        ],
        compiler_params=params(0),
        name="exchange",
    )(direction, block_pairs, depth_band.reshape(cells // 128, 128), station_offsets)

    img, pair_list, count = pl.pallas_call(
        forward_kernel,
        out_shape=(
            shape((slots + 1, epochs, SBLOCK), F32),
            shape((slots * pairs + UNROLL,), jnp.int32),
            shape((1,), jnp.int32),
        ),
        in_specs=[smem, vmem, vmem, vmem],
        out_specs=(vmem, smem, smem),
        compiler_params=params(),
        name="forward",
    )(codes, st, z, v)

    newres, scal = pl.pallas_call(
        functools.partial(image_kernel, n, rows),
        out_shape=(shape((slots, epochs, SBLOCK), F32), shape((8, 128), F32)),
        in_specs=[vmem] * 4,
        out_specs=(vmem,) * 2,
        scratch_shapes=[
            pltpu.VMEM((rows, epochs, SBLOCK), F32),
            pltpu.VMEM((rows, epochs, SBLOCK), F32),
            pltpu.VMEM((3, rows, epochs, SBLOCK), F32),
            pltpu.VMEM((8, 128), F32),
            pltpu.VMEM((n, 8, 128), F32),
            dma((8,)),
            dma((8,)),
            dma((n,)),
            dma((n,)),
        ],
        compiler_params=params(1),
        name="images",
    )(img, residual, norm, old_grad)

    new_model, gradient, gamma, new_residual = pl.pallas_call(
        adjoint_kernel,
        out_shape=(
            shape((epochs, cells), F32),
            shape((epochs, cells), F32),
            shape((8, 128), F32),
            shape((epochs, stations), F32),
        ),
        in_specs=[smem, smem] + [vmem] * 7,
        out_specs=(pl.BlockSpec(memory_space=pltpu.HBM),) + (vmem,) * 3,
        scratch_shapes=[
            pltpu.VMEM((blocks, epochs, CBLOCK), F32),
            pltpu.VMEM((slots + 1, 2 * epochs, SBLOCK), BF16),
            pltpu.VMEM((epochs, cells), F32),
            dma(()),
        ],
        compiler_params=params(),
        name="adjoint",
    )(pair_list, count, st, z, f, newres, scal, model_field, direction)

    ratio = pl.pallas_call(
        functools.partial(gamma_kernel, n),
        out_shape=shape((1, 1), F32),
        in_specs=[vmem] * 2,
        out_specs=vmem,
        scratch_shapes=[pltpu.VMEM((n, 8, 128), F32), dma((n,)), dma((n,))],
        compiler_params=params(2),
        name="gamma",
    )(gamma, scal)
    new_direction = gradient + ratio.reshape(()) * direction
    return (new_model, new_residual, new_direction)


def solution(mesh):
    both = ("groups", "tile")
    wide = P(None, both)
    return jax.shard_map(
        shards,
        mesh=mesh,
        in_specs=(wide, wide, wide, wide, P(both, None), P(both), wide),
        out_specs=(wide, wide, wide),
        check_vma=False,
    )
```

profile of v0, /device:TPU:0, one launch (start us, length us, event | category | flops | bytes accessed | tf_op | source)
XLA Modules:
  0.0 79.3 jit_solution(3499984777183754399)
XLA Ops:
  0.6 0.0 copy-start
  0.6 1.2 %copy-done = f32[16,16384]{1,0:T(8,128)S(1)} copy-done((f32[16,16384]{1,0:T(8,128)S(1)}, f32[16,16384]{1,0:T(8,128)}, u32[]{:S(2)}) %copy-start) | copy-done | bytes 1048600
  1.9 0.0 copy-start.5
  1.9 0.8 %copy-done.5 = s32[16384]{0:T(1024)S(1)} copy-done((s32[16384]{0:T(1024)S(1)}, s32[16384]{0:T(1024)}, u32[]{:S(2)}) %copy-start.5) | copy-done | bytes 65560
  2.7 0.0 copy-start.6
  2.7 0.7 copy-done.6
  3.4 0.0 copy-start.7
  3.4 0.7 copy-done.7
  4.1 0.0 copy-start.2
  4.1 6.4 %exchange.1 = (f32[40,2,256]{2,1,0:T(2,128)S(1)}, s32[5,8,8]{2,1,0:T(8,128)S(1)}, bf16[32,32,512]{2,1,0:T(8,128)(2,1)S(1)}, f32[128,128]{1,0:T(8,128)S(1)}, f32[...) custom-call(f32[16,16384]{1,0:T(8,128)S(1)} %copy-done, s32[8,8]{1,0:T(8,128)S(1)} %copy-done.7, s32[128,128]{1,0:T(8,128)S(1)} %bitcast.2, ...), custom_call_target="tpu_custom_call" | custom-call | tf_op jit(solution)/shard_map/exchange/pallas_call | solution.py:412
  10.5 0.0 copy-start.4
  10.5 0.0 copy-start.3
  10.5 11.6 %forward.1 = (f32[41,16,256]{2,1,0:T(8,128)S(1)}, s32[328]{0:T(512)S(1)}, s32[1]{0:T(128)}) custom-call(s32[5,8,8]{2,1,0:T(8,128)S(1)} %get-tuple-element.18.codes, f32[40,2,256]{2,1,0:T(2,128)S(1)} %get-tuple-element.19.st, f32[128,128]{1,0:T(8,128)S(1)} %get-tuple-element.20.z, bf16[32,32,512]{2,1,0:T(8,128)(2,1)S(1)} %get-tuple-element.21.v), custom_call_target="tpu_custom_call" | custom-call | tf_op jit(solution)/shard_map/forward/pallas_call | solution.py:432
  22.2 0.0 copy-start.1
  22.2 0.0 copy-done.2
  22.2 0.0 copy-done.4
  22.2 26.3 %images.1 = (f32[40,16,256]{2,1,0:T(8,128)S(1)}, f32[8,128]{1,0:T(8,128)S(1)}) custom-call(f32[41,16,256]{2,1,0:T(8,128)S(1)} %get-tuple-element.25.img, f32[16,2048]{1,0:T(8,128)S(1)} %copy-done.4, f32[8,128]{1,0:T(8,128)S(1)} %get-tuple-element.26.norm, f32[16,16384]{1,0:T(8,128)S(1)} %copy-done.2), custom_call_target="tpu_custom_call" | custom-call | tf_op jit(solution)/shard_map/images/pallas_call | solution.py:445
  48.6 0.0 copy-done.3
  48.6 0.0 copy-done.1
  48.6 13.3 %adjoint.1 = (f32[16,16384]{1,0:T(8,128)}, f32[16,16384]{1,0:T(8,128)S(1)}, f32[8,128]{1,0:T(8,128)S(1)}, f32[16,2048]{1,0:T(8,128)}) custom-call(s32[328]{0:T(512)S(1)} %get-tuple-element.22.pair_list, s32[1]{0:T(128)} %get-tuple-element.23.count, f32[40,2,256]{2,1,0:T(2,128)S(1)} %get-tuple-element.19.st, f32[128,128]{1,0:T(8,128)S(1)} %get-tuple-element.20.z, ...), custom_call_target="tpu_custom_call" | custom-call | tf_op jit(solution)/shard_map/adjoint/pallas_call | solution.py:465
  61.8 15.7 %gamma.1 = f32[1,1]{1,0:T(1,128)} custom-call(f32[8,128]{1,0:T(8,128)S(1)} %get-tuple-element.32.gamma, f32[8,128]{1,0:T(8,128)S(1)} %get-tuple-element.28.scal), custom_call_target="tpu_custom_call" | custom-call | tf_op jit(solution)/shard_map/gamma/pallas_call | solution.py:485
  77.6 1.7 %multiply_add_fusion = f32[16,16384]{1,0:T(8,128)} fusion(f32[16,16384]{1,0:T(8,128)S(1)} %get-tuple-element.31, f32[16,16384]{1,0:T(8,128)S(1)} %copy-done.1, f32[]{:T(128)} %bitcast.1), kind=kLoop, calls=%fused_computation | loop fusion | flops 524288 | bytes 3145732 | tf_op jit(solution)/shard_map/add | solution.py:494
Async XLA Ops:
  0.6 1.2 %copy-start = (f32[16,16384]{1,0:T(8,128)S(1)}, f32[16,16384]{1,0:T(8,128)}, u32[]{:S(2)}) copy-start(f32[16,16384]{1,0:T(8,128)} %dirn.3) | copy-start | bytes 3145732
  1.9 0.8 %copy-start.5 = (s32[16384]{0:T(1024)S(1)}, s32[16384]{0:T(1024)}, u32[]{:S(2)}) copy-start(s32[16384]{0:T(1024)} %param.12) | copy-start | bytes 196612
  2.7 0.7 copy-start.6
  3.4 0.7 copy-start.7
  4.1 18.1 %copy-start.2 = (f32[16,16384]{1,0:T(8,128)S(1)}, f32[16,16384]{1,0:T(8,128)}, u32[]{:S(2)}) copy-start(f32[16,16384]{1,0:T(8,128)} %old.1) | copy-start | bytes 3145732
  10.5 11.7 %copy-start.4 = (f32[16,2048]{1,0:T(8,128)S(1)}, f32[16,2048]{1,0:T(8,128)}, u32[]{:S(2)}) copy-start(f32[16,2048]{1,0:T(8,128)} %res.1) | copy-start | bytes 393220
  10.5 38.0 %copy-start.3 = (f32[16,16384]{1,0:T(8,128)S(1)}, f32[16,16384]{1,0:T(8,128)}, u32[]{:S(2)}) copy-start(f32[16,16384]{1,0:T(8,128)} %model.1) | copy-start | bytes 3145732
  22.2 26.4 %copy-start.1 = (f32[16,16384]{1,0:T(8,128)S(1)}, f32[16,16384]{1,0:T(8,128)}, u32[]{:S(2)}) copy-start(f32[16,16384]{1,0:T(8,128)} %dirn.3) | copy-start | bytes 3145732
where the time goes:
time: 78.1 us; the launch traced here: 79.3 us
  Pallas kernels  73.4 us (94%)
  local copies, waits for them, and re-layouts  3.48 us (4%)
  other arithmetic  1.73 us (2%)
    pallas_call x1, Pallas kernels, shards(): pl.pallas_call(functools.partial(image_kernel, n, rows), out_shape=(shape...  26.3 us
    pallas_call x1, Pallas kernels, shards(): pl.pallas_call(functools.partial(gamma_kernel, n), out_shape=shape((1, 1)...  15.7 us
    pallas_call x1, Pallas kernels, shards(): pl.pallas_call(adjoint_kernel, out_shape=(shape((epochs, cells), F32), sh...  13.3 us
    pallas_call x1, Pallas kernels, shards(): pl.pallas_call(forward_kernel, out_shape=(shape((slots + 1, epochs, SBLOC...  11.6 us
    pallas_call x1, Pallas kernels, shards(): pl.pallas_call(functools.partial(exchange_kernel, n, scale, blocks), out_...  6.39 us
    unnamed x16, local copies, waits for them, and re-layouts  3.48 us
    add x1, other arithmetic, shards(): new_direction = gradient + ratio.reshape(()) * direction  1.73 us

commit v1 on v0

--- a/solution.py
+++ b/solution.py
@@ -21,10 +21,11 @@
 SPAN = 2 * REACH + 1
 HOPS = tuple(r for r in range(-REACH, REACH + 1) if r != 0)
 UNROLL = 8
+KEPT = 88
 MESH = pl.DeviceIdType.MESH
 F32 = jnp.float32
 BF16 = jnp.bfloat16
-VMEM_LIMIT = 48 * 1024 * 1024
+VMEM_LIMIT = 6 * 1024 * 1024
 
 
 def exists(me, r, n):
@@ -152,7 +153,7 @@
     return j, b, halves
 
 
-def forward_kernel(codes, st, z, v, img, pair_list, count):
+def forward_kernel(codes, st, z, v, img, pair_list, count, *kept):
     rows = codes.shape[1]
     img[...] = jnp.zeros(img.shape, F32)
     filled = jnp.int32(0)
@@ -169,19 +170,23 @@
         pair_list[filled + u] = SPAN * rows * 32
     steps = (filled + (UNROLL - 1)) // UNROLL
     count[0] = steps
-
-    def step(i, carry):
+    count[1] = jnp.minimum(steps, KEPT // UNROLL)
+
+    def step(keep, i, carry):
         for u in range(UNROLL):
             j, b, halves = kernel_halves(pair_list[i * UNROLL + u], st, z)
             out = jnp.zeros((32, SBLOCK), F32)
             for h in range(2):
                 values = v[b, :, h * 256 : (h + 1) * 256]
-                for part in halves[h]:
+                for w, part in enumerate(halves[h]):
+                    if keep:
+                        kept[u][i, h, w] = part
                     out = out + jnp.dot(values, part, preferred_element_type=F32)
             img[j] += out[0:16] + out[16:32]
         return carry
 
-    lax.fori_loop(0, steps, step, 0)
+    lax.fori_loop(0, count[1], functools.partial(step, True), 0)
+    lax.fori_loop(count[1], steps, functools.partial(step, False), 0)
 
 
 def all_sum(n, me, mine, landing, send_sem, recv_sem, start, finish):
@@ -322,9 +327,10 @@
 
 
 def adjoint_kernel(
-    pair_list, count, st, z, f, newres, scal, model, dirn,
-    model_hbm, grad_o, gamma_o, res_o, acc, parts, model_o, out_sem,
+    pair_list, count, st, z, f, newres, scal, model, dirn, *rest,
 ):
+    kept = rest[:UNROLL]
+    model_hbm, grad_o, gamma_o, res_o, acc, parts, model_o, out_sem = rest[UNROLL:]
     slots = newres.shape[0]
     rows = slots // SPAN
     for k in range(rows):
@@ -349,20 +355,30 @@
     parts[slots] = jnp.zeros((32, SBLOCK), BF16)
     acc[...] = jnp.zeros(acc.shape, F32)
 
-    def step(i, carry):
+    def add_pair(j, b, halves):
+        values = parts[j]
+        for h in range(2):
+            out = jnp.zeros((32, 256), F32)
+            for part in halves[h]:
+                out = out + lax.dot_general(
+                    values, part, (((1,), (1,)), ((), ())), preferred_element_type=F32
+                )
+            acc[b, :, h * 256 : (h + 1) * 256] += out[0:16] + out[16:32]
+
+    def reread(i, carry):
         for u in range(UNROLL):
-            j, b, halves = kernel_halves(pair_list[i * UNROLL + u], st, z)
-            values = parts[j]
-            for h in range(2):
-                out = jnp.zeros((32, 256), F32)
-                for part in halves[h]:
-                    out = out + lax.dot_general(
-                        values, part, (((1,), (1,)), ((), ())), preferred_element_type=F32
-                    )
-                acc[b, :, h * 256 : (h + 1) * 256] += out[0:16] + out[16:32]
+            entry = pair_list[i * UNROLL + u]
+            halves = [[kept[u][i, h, w] for w in range(2)] for h in range(2)]
+            add_pair(lax.shift_right_logical(entry, 5), lax.bitwise_and(entry, 31), halves)
         return carry
 
-    lax.fori_loop(0, count[0], step, 0)
+    def rebuild(i, carry):
+        for u in range(UNROLL):
+            add_pair(*kernel_halves(pair_list[i * UNROLL + u], st, z))
+        return carry
+
+    lax.fori_loop(0, count[1], reread, 0)
+    lax.fori_loop(count[1], count[0], rebuild, 0)
 
     def finish(b, total):
         lanes = pl.ds(pl.multiple_of(b * CBLOCK, CBLOCK), CBLOCK)
@@ -429,19 +445,20 @@
         name="exchange",
     )(direction, block_pairs, depth_band.reshape(cells // 128, 128), station_offsets)
 
-    img, pair_list, count = pl.pallas_call(
+    img, pair_list, count, *kept = pl.pallas_call(
         forward_kernel,
         out_shape=(
             shape((slots + 1, epochs, SBLOCK), F32),
             shape((slots * pairs + UNROLL,), jnp.int32),
-            shape((1,), jnp.int32),
-        ),
+            shape((2,), jnp.int32),
+        ) + (pltpu.VMEM((KEPT // UNROLL, 2, 2, 256, SBLOCK), BF16),) * UNROLL,
         in_specs=[smem, vmem, vmem, vmem],
-        out_specs=(vmem, smem, smem),
+        out_specs=(vmem, smem, smem) + (vmem,) * UNROLL,
         compiler_params=params(),
         name="forward",
     )(codes, st, z, v)
 
+    kept = [pltpu.with_memory_space_constraint(k, pltpu.VMEM) for k in kept]
     newres, scal = pl.pallas_call(
         functools.partial(image_kernel, n, rows),
         out_shape=(shape((slots, epochs, SBLOCK), F32), shape((8, 128), F32)),
@@ -470,7 +487,7 @@
             shape((8, 128), F32),
             shape((epochs, stations), F32),
         ),
-        in_specs=[smem, smem] + [vmem] * 7,
+        in_specs=[smem, smem] + [vmem] * (7 + UNROLL),
         out_specs=(pl.BlockSpec(memory_space=pltpu.HBM),) + (vmem,) * 3,
         scratch_shapes=[
             pltpu.VMEM((blocks, epochs, CBLOCK), F32),
@@ -480,7 +497,7 @@
         ],
         compiler_params=params(),
         name="adjoint",
-    )(pair_list, count, st, z, f, newres, scal, model_field, direction)
+    )(pair_list, count, st, z, f, newres, scal, model_field, direction, *kept)
 
     ratio = pl.pallas_call(
         functools.partial(gamma_kernel, n),

time: 78.1 us -> 81.7 us (1.046)
  the two profiles are of different devices: /device:TPU:0 before, /device:TPU:3 now
where the time goes in v1:
time: 81.7 us; the launch traced here: 80.8 us
  Pallas kernels  70.3 us (86%)
  local copies, waits for them, and re-layouts  8.03 us (10%)
  other arithmetic  1.74 us (2%)
    pallas_call x1, Pallas kernels, shards(): pl.pallas_call(functools.partial(image_kernel, n, rows), out_shape=(shape...  23.8 us
    pallas_call x1, Pallas kernels, shards(): pl.pallas_call(forward_kernel, out_shape=(shape((slots + 1, epochs, SBLOC...  16.2 us
    pallas_call x1, Pallas kernels, shards(): pl.pallas_call(adjoint_kernel, out_shape=(shape((epochs, cells), F32), sh...  13.6 us
    pallas_call x1, Pallas kernels, shards(): pl.pallas_call(functools.partial(gamma_kernel, n), out_shape=shape((1, 1)...  11.5 us
    unnamed x18, local copies, waits for them, and re-layouts  8.03 us
    pallas_call x1, Pallas kernels, shards(): pl.pallas_call(functools.partial(exchange_kernel, n, scale, blocks), out_...  5.23 us
    add x1, other arithmetic, shards(): new_direction = gradient + ratio.reshape(()) * direction  1.74 us

profile of v1, /device:TPU:3, one launch (start us, length us, event | category | flops | bytes accessed | tf_op | source)
XLA Modules:
  0.0 80.8 jit_solution(10112501970169559855)
XLA Ops:
  0.6 0.0 copy-start
  0.6 1.2 %copy-done = f32[16,16384]{1,0:T(8,128)S(1)} copy-done((f32[16,16384]{1,0:T(8,128)S(1)}, f32[16,16384]{1,0:T(8,128)}, u32[]{:S(2)}) %copy-start) | copy-done | bytes 1048600
  1.9 0.0 copy-start.6
  1.9 0.8 %copy-done.6 = s32[16384]{0:T(1024)S(1)} copy-done((s32[16384]{0:T(1024)S(1)}, s32[16384]{0:T(1024)}, u32[]{:S(2)}) %copy-start.6) | copy-done | bytes 65560
  2.7 0.0 copy-start.7
  2.7 0.7 copy-done.7
  3.4 0.0 copy-start.8
  3.4 0.7 copy-done.8
  4.1 5.2 %exchange.1 = (f32[40,2,256]{2,1,0:T(2,128)S(1)}, s32[5,8,8]{2,1,0:T(8,128)S(1)}, bf16[32,32,512]{2,1,0:T(8,128)(2,1)S(1)}, f32[128,128]{1,0:T(8,128)S(1)}, f32[...) custom-call(f32[16,16384]{1,0:T(8,128)S(1)} %copy-done, s32[8,8]{1,0:T(8,128)S(1)} %copy-done.8, s32[128,128]{1,0:T(8,128)S(1)} %bitcast.2, ...), custom_call_target="tpu_custom_call" | custom-call | tf_op jit(solution)/shard_map/exchange/pallas_call | solution.py:428
  9.3 16.2 %forward.1 = (f32[41,16,256]{2,1,0:T(8,128)S(1)}, s32[328]{0:T(512)S(1)}, s32[2]{0:T(128)S(1)}, bf16[11,2,2,256,256]{4,3,2,1,0:T(8,128)(2,1)S(1)}, bf16[11,2,2,2...) custom-call(s32[5,8,8]{2,1,0:T(8,128)S(1)} %get-tuple-element.26.cod, ...), custom_call_target="tpu_custom_call" | custom-call | tf_op jit(solution)/shard_map/forward/pallas_call | solution.py:448
  25.5 0.0 copy-start.4
  25.6 1.2 %copy-done.4 = f32[16,16384]{1,0:T(8,128)S(1)} copy-done((f32[16,16384]{1,0:T(8,128)S(1)}, f32[16,16384]{1,0:T(8,128)}, u32[]{:S(2)}) %copy-start.4) | copy-done | bytes 1048600
  26.8 0.0 copy-start.5
  26.8 0.9 %copy-done.5 = f32[16,2048]{1,0:T(8,128)S(1)} copy-done((f32[16,2048]{1,0:T(8,128)S(1)}, f32[16,2048]{1,0:T(8,128)}, u32[]{:S(2)}) %copy-start.5) | copy-done | bytes 131096
  27.7 23.8 %images.1 = (f32[40,16,256]{2,1,0:T(8,128)S(1)}, f32[8,128]{1,0:T(8,128)S(1)}) custom-call(f32[41,16,256]{2,1,0:T(8,128)S(1)} %get-tuple-element.33.img, f32[16,2048]{1,0:T(8,128)S(1)} %copy-done.5, f32[8,128]{1,0:T(8,128)S(1)} %get-tuple-element.34.norm, f32[16,16384]{1,0:T(8,128)S(1)} %copy-done.4), custom_call_target="tpu_custom_call" | custom-call | tf_op jit(solution)/shard_map/images/pallas_call | solution.py:462
  51.5 0.0 copy-start.1
  51.5 1.2 %copy-done.1 = f32[16,16384]{1,0:T(8,128)S(1)} copy-done((f32[16,16384]{1,0:T(8,128)S(1)}, f32[16,16384]{1,0:T(8,128)}, u32[]{:S(2)}) %copy-start.1) | copy-done | bytes 1048600
  52.7 0.0 copy-start.3
  52.7 1.2 %copy-done.3 = f32[16,16384]{1,0:T(8,128)S(1)} copy-done((f32[16,16384]{1,0:T(8,128)S(1)}, f32[16,16384]{1,0:T(8,128)}, u32[]{:S(2)}) %copy-start.3) | copy-done | bytes 1048600
  53.9 0.0 copy-start.2
  53.9 13.6 %adjoint.1 = (f32[16,16384]{1,0:T(8,128)}, f32[16,16384]{1,0:T(8,128)S(1)}, f32[8,128]{1,0:T(8,128)S(1)}, f32[16,2048]{1,0:T(8,128)}) custom-call(s32[328]{0:T(512)S(1)} %get-tuple-element.30.pair_list, s32[2]{0:T(128)S(1)} %get-tuple-element.31.count, f32[40,2,256]{2,1,0:T(2,128)S(1)} %get-tuple-element.27.st, f32[128,128]{1,0:T(8,128)S(1)} %get-tuple-element.28.z, ...), custom_call_target="tpu_custom_call" | custom-call | tf_op jit(solution)/shard_map/adjoint/pallas_call | solution.py:482
  67.6 11.5 %gamma.1 = f32[1,1]{1,0:T(1,128)} custom-call(f32[8,128]{1,0:T(8,128)S(1)} %get-tuple-element.48.gamma, f32[8,128]{1,0:T(8,128)S(1)} %get-tuple-element.36.scal), custom_call_target="tpu_custom_call" | custom-call | tf_op jit(solution)/shard_map/gamma/pallas_call | solution.py:502
  79.1 0.0 copy-done.2
  79.1 1.7 %multiply_add_fusion = f32[16,16384]{1,0:T(8,128)} fusion(f32[16,16384]{1,0:T(8,128)S(1)} %get-tuple-element.47, f32[16,16384]{1,0:T(8,128)S(1)} %copy-done.2, f32[]{:T(128)} %bitcast.1), kind=kLoop, calls=%fused_computation | loop fusion | flops 524288 | bytes 3145732 | tf_op jit(solution)/shard_map/add | solution.py:511
Async XLA Ops:
  0.6 1.2 %copy-start = (f32[16,16384]{1,0:T(8,128)S(1)}, f32[16,16384]{1,0:T(8,128)}, u32[]{:S(2)}) copy-start(f32[16,16384]{1,0:T(8,128)} %dirn.3) | copy-start | bytes 3145732
  1.9 0.8 %copy-start.6 = (s32[16384]{0:T(1024)S(1)}, s32[16384]{0:T(1024)}, u32[]{:S(2)}) copy-start(s32[16384]{0:T(1024)} %param.12) | copy-start | bytes 196612
  2.7 0.7 copy-start.7
  3.4 0.7 copy-start.8
  25.5 1.2 %copy-start.4 = (f32[16,16384]{1,0:T(8,128)S(1)}, f32[16,16384]{1,0:T(8,128)}, u32[]{:S(2)}) copy-start(f32[16,16384]{1,0:T(8,128)} %old.1) | copy-start | bytes 3145732
  26.8 0.9 %copy-start.5 = (f32[16,2048]{1,0:T(8,128)S(1)}, f32[16,2048]{1,0:T(8,128)}, u32[]{:S(2)}) copy-start(f32[16,2048]{1,0:T(8,128)} %res.1) | copy-start | bytes 393220
  51.5 1.2 %copy-start.1 = (f32[16,16384]{1,0:T(8,128)S(1)}, f32[16,16384]{1,0:T(8,128)}, u32[]{:S(2)}) copy-start(f32[16,16384]{1,0:T(8,128)} %dirn.3) | copy-start | bytes 3145732
  52.7 1.2 %copy-start.3 = (f32[16,16384]{1,0:T(8,128)S(1)}, f32[16,16384]{1,0:T(8,128)}, u32[]{:S(2)}) copy-start(f32[16,16384]{1,0:T(8,128)} %model.1) | copy-start | bytes 3145732
  53.9 25.1 %copy-start.2 = (f32[16,16384]{1,0:T(8,128)S(1)}, f32[16,16384]{1,0:T(8,128)}, u32[]{:S(2)}) copy-start(f32[16,16384]{1,0:T(8,128)} %dirn.3) | copy-start | bytes 3145732

commit v2 on v0

--- a/solution.py
+++ b/solution.py
@@ -19,8 +19,9 @@
 GUARD = 1e-06
 
 SPAN = 2 * REACH + 1
+CHUNKS = 4
 HOPS = tuple(r for r in range(-REACH, REACH + 1) if r != 0)
-UNROLL = 8
+UNROLL = 4
 MESH = pl.DeviceIdType.MESH
 F32 = jnp.float32
 BF16 = jnp.bfloat16
@@ -45,11 +46,26 @@
 
 
 def exchange_kernel(
-    n, scale, blocks, dirn, pairs, band, offs,
-    st_o, codes_o, v_o, f_o, z_o, norm_o, send_sem, recv_sem,
+    n, scale, blocks, dirn_hbm, pairs, band_hbm, offs_hbm,
+    st_o, codes_o, v_o, f_o, z_o, norm_o,
+    dirn, band, offs, in_sem, send_sem, recv_sem,
 ):
     me = lax.axis_index("tile")
     rows = pairs.shape[0]
+    part = dirn.shape[1] // CHUNKS
+    fetch_offs = pltpu.make_async_copy(offs_hbm, offs, in_sem.at[0])
+    fetch_pairs = pltpu.make_async_copy(pairs, codes_o.at[REACH], in_sem.at[1])
+    fetch_band = pltpu.make_async_copy(band_hbm, band, in_sem.at[2])
+    fetch_dirn = [
+        pltpu.make_async_copy(
+            dirn_hbm.at[:, k * part : (k + 1) * part],
+            dirn.at[:, k * part : (k + 1) * part],
+            in_sem.at[3 + k],
+        )
+        for k in range(CHUNKS)
+    ]
+    for one in [fetch_offs, fetch_pairs, fetch_band] + fetch_dirn:
+        one.start()
     barrier = pltpu.get_barrier_semaphore()
     for r in HOPS:
         @pl.when(exists(me, r, n))
@@ -57,15 +73,16 @@
             pl.semaphore_signal(barrier, inc=1, device_id={"tile": me + r}, device_id_type=MESH)
 
     own = REACH * rows
-    for k in range(rows):
-        st_o[own + k] = offs[:, k * SBLOCK : (k + 1) * SBLOCK]
-    codes_o[REACH] = pairs[...]
     for r in HOPS:
         @pl.when(jnp.logical_not(exists(me, r, n)))
         def _():
             t = r + REACH
             st_o[t * rows : (t + 1) * rows] = jnp.zeros((rows,) + st_o.shape[1:], F32)
             codes_o[t] = jnp.full(codes_o.shape[1:], -1, jnp.int32)
+    fetch_offs.wait()
+    for k in range(rows):
+        st_o[own + k] = offs[:, k * SBLOCK : (k + 1) * SBLOCK]
+    fetch_pairs.wait()
 
     peers = sum(exists(me, r, n).astype(jnp.int32) for r in HOPS)
     pl.semaphore_wait(barrier, peers)
@@ -89,6 +106,7 @@
             for one in copies(q, r):
                 one.start()
 
+    fetch_band.wait()
     depth = (band[...].astype(F32) + 0.5) * (DEPTH_RANGE / BANDS)
     shifted = depth + DEPTH_SHIFT
     f_o[...] = scale * depth * (shifted * jnp.sqrt(shifted))
@@ -104,10 +122,11 @@
             total = total + values * values
         return total
 
-    total = lax.fori_loop(0, blocks, block, jnp.zeros((dirn.shape[0], 128), F32))
-    norm_o[...] = jnp.concatenate(
-        [jnp.zeros((1, 128), F32), lane_sums(total), jnp.zeros((6, 128), F32)], axis=0
-    )
+    total = jnp.zeros((dirn.shape[0], 128), F32)
+    for k in range(CHUNKS):
+        fetch_dirn[k].wait()
+        total = lax.fori_loop(k * blocks // CHUNKS, (k + 1) * blocks // CHUNKS, block, total)
+    norm_o[...] = jnp.broadcast_to(lane_sums(total), norm_o.shape)
 
     for q, r in enumerate(HOPS):
         @pl.when(exists(me, r, n))
@@ -129,10 +148,10 @@
     moved = (at // rows - REACH).astype(F32)
     parity = lax.bitwise_and(b, 1).astype(F32)
     place = st[at]
-    sx = place[0:1, :] + moved
-    sy = place[1:2, :] - 0.5 * parity
+    sx = jnp.broadcast_to(place[0:1, :] + moved, (8, SBLOCK))
+    sy = jnp.broadcast_to(place[1:2, :] - 0.5 * parity, (8, SBLOCK))
     column = (lax.broadcasted_iota(jnp.int32, (COL_SIDE, SBLOCK), 0).astype(F32) + 0.5) / COL_SIDE
-    across = sx - column
+    across = jnp.concatenate([sx] * (COL_SIDE // 8), axis=0) - column
     across = across * across
     which = jnp.full((COL_SIDE, 128), b * (CBLOCK // 128), jnp.int32)
     halves = []
@@ -140,7 +159,7 @@
         highs, lows = [], []
         for a in range(h * 8, h * 8 + 8):
             along = sy - (a + 0.5) / COL_SIDE
-            along = along * along
+            along = jnp.concatenate([along * along] * (COL_SIDE // 8), axis=0)
             low_row = a % 4 * COL_SIDE
             picked = jnp.take_along_axis(z[low_row : low_row + COL_SIDE, :], which + a // 4, axis=1)
             picked = jnp.concatenate([picked, picked], axis=1)
@@ -202,16 +221,19 @@
         lax.fori_loop(1, n, done, 0)
 
 
-def greet_all(n, me):
+def greet(n, me):
     barrier = pltpu.get_barrier_semaphore()
 
-    def greet(k, c):
+    def one(k, c):
         pl.semaphore_signal(
             barrier, inc=1, device_id={"tile": lax.rem(me + k, n)}, device_id_type=MESH
         )
         return c
-    lax.fori_loop(1, n, greet, 0)
-    pl.semaphore_wait(barrier, n - 1)
+    lax.fori_loop(1, n, one, 0)
+
+
+def greeted(n):
+    pl.semaphore_wait(pltpu.get_barrier_semaphore(), n - 1)
 
 
 def image_kernel(
@@ -219,7 +241,8 @@
     transit, joined, part_rx, norm_tx, norm_rx, send_sem, recv_sem, nsend_sem, nrecv_sem,
 ):
     me = lax.axis_index("tile")
-    greet_all(n, me)
+    greet(n, me)
+    greeted(n)
     s = 1 - 2 * lax.rem(me, 2)
     outward = exists(me, -2 * s, n)
     inward = exists(me, 2 * s, n)
@@ -257,8 +280,10 @@
         return total + values * values
 
     before = lax.fori_loop(0, old.shape[1] // 512, squares, jnp.zeros((old.shape[0], 512), F32))
-    norm_tx[...] = norm[...]
-    norm_tx[0:1, :] = lane_sums(before)
+    lane = lax.broadcasted_iota(jnp.int32, (1, 128), 1)
+    gamma_part = jnp.sum(lane_sums(before), axis=1, keepdims=True)
+    norm_part = DAMPING * jnp.sum(norm[0:1, :], axis=1, keepdims=True)
+    known = jnp.where(lane == 0, gamma_part, jnp.where(lane == 1, norm_part, 0.0))
 
     @pl.when(outward)
     def _():
@@ -281,12 +306,15 @@
         newres_o[here : here + rows] += part_rx[2]
 
     image = newres_o[here : here + rows]
-    norm_tx[2:3, :] = lane_sums(jnp.sum(image * image, axis=0))
+    squared = lane_sums(jnp.sum(image * image, axis=0))
+    folded = squared + jnp.where(lane == 1, 0.0, pltpu.roll(jnp.where(lane < 2, squared, 0.0), 2, 1))
+    norm_tx[...] = jnp.where(lane < 2, known, folded)
     all_sum(n, me, norm_tx, norm_rx, nsend_sem, nrecv_sem, True, True)
     norm_rx[0] = norm_tx[...]
-    totals = jnp.sum(jnp.sum(norm_rx[...], axis=0), axis=1, keepdims=True)
-    gamma_old = totals[0:1]
-    length = gamma_old / (totals[2:3] + DAMPING * totals[1:2] + GUARD)
+    totals = jnp.sum(norm_rx[...], axis=0)
+    gamma_old = jnp.sum(jnp.where(lane == 0, totals, 0.0), axis=1, keepdims=True)
+    curvature = jnp.sum(jnp.where(lane == 0, 0.0, totals), axis=1, keepdims=True)
+    length = gamma_old / (curvature + GUARD)
     scal_o[...] = jnp.concatenate(
         [jnp.broadcast_to(length, (4, 128)), jnp.broadcast_to(gamma_old, (4, 128))], axis=0
     )
@@ -322,8 +350,8 @@
 
 
 def adjoint_kernel(
-    pair_list, count, st, z, f, newres, scal, model, dirn,
-    model_hbm, grad_o, gamma_o, res_o, acc, parts, model_o, out_sem,
+    pair_list, count, st, z, newres, scal, model, dirn,
+    model_hbm, model_o, acc, res_o, parts, out_sem,
 ):
     slots = newres.shape[0]
     rows = slots // SPAN
@@ -364,27 +392,28 @@
 
     lax.fori_loop(0, count[0], step, 0)
 
+    leave.wait()
+
+
+def gamma_kernel(n, acc, model, f, scal, grad_o, ratio_o, mine, landing, send_sem, recv_sem):
+    me = lax.axis_index("tile")
+    greet(n, me)
+
     def finish(b, total):
         lanes = pl.ds(pl.multiple_of(b * CBLOCK, CBLOCK), CBLOCK)
-        new_model = model_o[:, lanes]
         factor = jnp.concatenate(
             [f[pl.ds(b * (CBLOCK // 128) + q, 1), :] for q in range(CBLOCK // 128)], axis=1
         )
-        gradient = factor * acc[b] - DAMPING * new_model
+        gradient = factor * acc[b] - DAMPING * model[:, lanes]
         grad_o[:, lanes] = gradient
         return total + gradient * gradient
 
     total = lax.fori_loop(0, acc.shape[0], finish, jnp.zeros((model.shape[0], CBLOCK), F32))
-    gamma_o[...] = jnp.concatenate([lane_sums(total), jnp.zeros((7, 128), F32)], axis=0)
-    leave.wait()
-
-
-def gamma_kernel(n, gamma, scal, ratio_o, landing, send_sem, recv_sem):
-    me = lax.axis_index("tile")
-    greet_all(n, me)
-    all_sum(n, me, gamma, landing, send_sem, recv_sem, True, True)
-    landing[0] = gamma[...]
-    total = jnp.sum(jnp.sum(landing[...], axis=0), axis=1, keepdims=True)[0:1]
+    mine[...] = lane_sums(total)
+    greeted(n)
+    all_sum(n, me, mine, landing, send_sem, recv_sem, True, True)
+    landing[0] = mine[...]
+    total = jnp.sum(jnp.sum(landing[...], axis=0), axis=1, keepdims=True)
     ratio_o[...] = total / (scal[4:5, 0:1] + GUARD)
 
 
@@ -398,6 +427,7 @@
     scale = 2.0 / math.sqrt(cells)
     vmem = pl.BlockSpec(memory_space=pltpu.VMEM)
     smem = pl.BlockSpec(memory_space=pltpu.SMEM)
+    hbm = pl.BlockSpec(memory_space=pltpu.HBM)
     shape = jax.ShapeDtypeStruct
     slots = SPAN * rows
     dma = pltpu.SemaphoreType.DMA
@@ -419,15 +449,22 @@
             shape((128, cells // 128), F32),
             shape((8, 128), F32),
         ),
-        in_specs=[vmem] * 4,
+        in_specs=[hbm] * 4,
         out_specs=(vmem,) * 6,
         scratch_shapes=[
+            pltpu.VMEM((epochs, cells), F32),
+            pltpu.VMEM((cells // 128, 128), jnp.int32),
+            pltpu.VMEM((2, stations), F32),
+            dma((3 + CHUNKS,)),
             dma((2, len(HOPS))),
             dma((2, len(HOPS))),
         ],
         compiler_params=params(0),
         name="exchange",
-    )(direction, block_pairs, depth_band.reshape(cells // 128, 128), station_offsets)
+    )(*(
+        pltpu.with_memory_space_constraint(one, pltpu.HBM)
+        for one in (direction, block_pairs, depth_band.reshape(cells // 128, 128), station_offsets)
+    ))
 
     img, pair_list, count = pl.pallas_call(
         forward_kernel,
@@ -451,8 +488,8 @@
             pltpu.VMEM((rows, epochs, SBLOCK), F32),
             pltpu.VMEM((rows, epochs, SBLOCK), F32),
             pltpu.VMEM((3, rows, epochs, SBLOCK), F32),
-            pltpu.VMEM((8, 128), F32),
-            pltpu.VMEM((n, 8, 128), F32),
+            pltpu.VMEM((1, 128), F32),
+            pltpu.VMEM((n, 1, 128), F32),
             dma((8,)),
             dma((8,)),
             dma((n,)),
@@ -462,35 +499,32 @@
         name="images",
     )(img, residual, norm, old_grad)
 
-    new_model, gradient, gamma, new_residual = pl.pallas_call(
+    new_model, model_kept, acc, new_residual = pl.pallas_call(
         adjoint_kernel,
         out_shape=(
             shape((epochs, cells), F32),
             shape((epochs, cells), F32),
-            shape((8, 128), F32),
+            shape((blocks, epochs, CBLOCK), F32),
             shape((epochs, stations), F32),
         ),
-        in_specs=[smem, smem] + [vmem] * 7,
-        out_specs=(pl.BlockSpec(memory_space=pltpu.HBM),) + (vmem,) * 3,
-        scratch_shapes=[
-            pltpu.VMEM((blocks, epochs, CBLOCK), F32),
-            pltpu.VMEM((slots + 1, 2 * epochs, SBLOCK), BF16),
-            pltpu.VMEM((epochs, cells), F32),
-            dma(()),
-        ],
+        in_specs=[smem, smem] + [vmem] * 6,
+        out_specs=(hbm,) + (vmem,) * 3,
+        scratch_shapes=[pltpu.VMEM((slots + 1, 2 * epochs, SBLOCK), BF16), dma(())],
         compiler_params=params(),
         name="adjoint",
-    )(pair_list, count, st, z, f, newres, scal, model_field, direction)
-
-    ratio = pl.pallas_call(
+    )(pair_list, count, st, z, newres, scal, model_field, direction)
+
+    gradient, ratio = pl.pallas_call(
         functools.partial(gamma_kernel, n),
-        out_shape=shape((1, 1), F32),
-        in_specs=[vmem] * 2,
-        out_specs=vmem,
-        scratch_shapes=[pltpu.VMEM((n, 8, 128), F32), dma((n,)), dma((n,))],
+        out_shape=(shape((epochs, cells), F32), shape((1, 1), F32)),
+        in_specs=[vmem] * 4,
+        out_specs=(vmem,) * 2,
+        scratch_shapes=[
+            pltpu.VMEM((1, 128), F32), pltpu.VMEM((n, 1, 128), F32), dma((n,)), dma((n,)),
+        ],
         compiler_params=params(2),
         name="gamma",
-    )(gamma, scal)
+    )(acc, model_kept, f, scal)
     new_direction = gradient + ratio.reshape(()) * direction
     return (new_model, new_residual, new_direction)
 

time: 78.1 us -> 79.2 us (1.014)
  Pallas kernels: 73.4 us -> 77.3 us
  local copies, waits for them, and re-layouts: 3.48 us -> 0.02 us
    unnamed x16 -> x8, local copies, waits for them, and re-layouts: 3.48 us -> 0.02 us
    pallas_call x1, Pallas kernels: 13.3 us -> 14.6 us  [shards(): pl.pallas_call(adjoint_kernel, out_shape=(shape((epochs, cells), F32), sh...]
    pallas_call x1, Pallas kernels: 11.6 us -> 12.8 us  [shards(): pl.pallas_call(forward_kernel, out_shape=(shape((slots + 1, epochs, SBLOC...]
    pallas_call x1, Pallas kernels: 15.7 us -> 16.8 us  [shards(): pl.pallas_call(functools.partial(gamma_kernel, n), out_shape=(shape((epoc...]
where the time goes in v2:
time: 79.2 us; the launch traced here: 79.8 us
  Pallas kernels  77.3 us (98%)
  other arithmetic  1.75 us (2%)
    pallas_call x1, Pallas kernels, shards(): pl.pallas_call(functools.partial(image_kernel, n, rows), out_shape=(shape...  26.6 us
    pallas_call x1, Pallas kernels, shards(): pl.pallas_call(functools.partial(gamma_kernel, n), out_shape=(shape((epoc...  16.8 us
    pallas_call x1, Pallas kernels, shards(): pl.pallas_call(adjoint_kernel, out_shape=(shape((epochs, cells), F32), sh...  14.6 us
    pallas_call x1, Pallas kernels, shards(): pl.pallas_call(forward_kernel, out_shape=(shape((slots + 1, epochs, SBLOC...  12.8 us
    pallas_call x1, Pallas kernels, shards(): pl.pallas_call(functools.partial(exchange_kernel, n, scale, blocks), out_...  6.5 us
    add x1, other arithmetic, shards(): new_direction = gradient + ratio.reshape(()) * direction  1.75 us

profile of v2, /device:TPU:0, one launch (start us, length us, event | category | flops | bytes accessed | tf_op | source)
XLA Modules:
  0.0 79.8 jit_solution(869229972923198318)
XLA Ops:
  0.6 0.0 copy-start.1
  0.6 6.5 %exchange.1 = (f32[40,2,256]{2,1,0:T(2,128)S(1)}, s32[5,8,8]{2,1,0:T(8,128)S(1)}, bf16[32,32,512]{2,1,0:T(8,128)(2,1)S(1)}, f32[128,128]{1,0:T(8,128)S(1)}, f32[...) custom-call(f32[16,16384]{1,0:T(8,128)} %dirn.1, s32[8,8]{1,0:T(8,128)} %pairs.1, s32[128,128]{1,0:T(8,128)} %bitcast.2, ...), custom_call_target="tpu_custom_call" | custom-call | tf_op jit(solution)/shard_map/exchange/pallas_call | solution.py:442
  7.1 0.0 copy-start.3
  7.2 0.0 copy-start.2
  7.2 12.8 %forward.1 = (f32[41,16,256]{2,1,0:T(8,128)S(1)}, s32[324]{0:T(512)S(1)}, s32[1]{0:T(128)}) custom-call(s32[5,8,8]{2,1,0:T(8,128)S(1)} %get-tuple-element.20.codes, f32[40,2,256]{2,1,0:T(2,128)S(1)} %get-tuple-element.21.st, f32[128,128]{1,0:T(8,128)S(1)} %get-tuple-element.22.z, bf16[32,32,512]{2,1,0:T(8,128)(2,1)S(1)} %get-tuple-element.23.v), custom_call_target="tpu_custom_call" | custom-call | tf_op jit(solution)/shard_map/forward/pallas_call | solution.py:469
  19.9 0.0 copy-start
  20.0 0.0 copy-done.1
  20.0 0.0 copy-done.3
  20.0 26.6 %images.1 = (f32[40,16,256]{2,1,0:T(8,128)S(1)}, f32[8,128]{1,0:T(8,128)S(1)}) custom-call(f32[41,16,256]{2,1,0:T(8,128)S(1)} %get-tuple-element.26.img, f32[16,2048]{1,0:T(8,128)S(1)} %copy-done.3, f32[8,128]{1,0:T(8,128)S(1)} %get-tuple-element.27.norm, f32[16,16384]{1,0:T(8,128)S(1)} %copy-done.1), custom_call_target="tpu_custom_call" | custom-call | tf_op jit(solution)/shard_map/images/pallas_call | solution.py:482
  46.6 0.0 copy-done.2
  46.6 0.0 copy-done
  46.6 14.6 %adjoint.1 = (f32[16,16384]{1,0:T(8,128)}, f32[16,16384]{1,0:T(8,128)S(1)}, f32[32,16,512]{2,1,0:T(8,128)S(1)}, f32[16,2048]{1,0:T(8,128)}) custom-call(s32[324]{0:T(512)S(1)} %get-tuple-element.24.pair_list, s32[1]{0:T(128)} %get-tuple-element.25.count, f32[40,2,256]{2,1,0:T(2,128)S(1)} %get-tuple-element.21.st, f32[128,128]{1,0:T(8,128)S(1)} %get-tuple-element.22.z, ...), custom_call_target="tpu_custom_call" | custom-call | tf_op jit(solution)/shard_map/adjoint/pallas_call | solution.py:502
  61.2 16.8 %gamma.1 = (f32[16,16384]{1,0:T(8,128)S(1)}, f32[1,1]{1,0:T(1,128)}) custom-call(f32[32,16,512]{2,1,0:T(8,128)S(1)} %get-tuple-element.32.acc, f32[16,16384]{1,0:T(8,128)S(1)} %get-tuple-element.33.model, f32[128,128]{1,0:T(8,128)S(1)} %get-tuple-element.34.f, f32[8,128]{1,0:T(8,128)S(1)} %get-tuple-element.29.scal), custom_call_target="tpu_custom_call" | custom-call | tf_op jit(solution)/shard_map/gamma/pallas_call | solution.py:517
  78.0 1.8 %multiply_add_fusion = f32[16,16384]{1,0:T(8,128)} fusion(f32[16,16384]{1,0:T(8,128)S(1)} %get-tuple-element.35, f32[16,16384]{1,0:T(8,128)S(1)} %copy-done, f32[]{:T(128)} %bitcast.1), kind=kLoop, calls=%fused_computation | loop fusion | flops 524288 | bytes 3145732 | tf_op jit(solution)/shard_map/add | solution.py:528
Async XLA Ops:
  0.6 19.3 %copy-start.1 = (f32[16,16384]{1,0:T(8,128)S(1)}, f32[16,16384]{1,0:T(8,128)}, u32[]{:S(2)}) copy-start(f32[16,16384]{1,0:T(8,128)} %old.1) | copy-start | bytes 3145732
  7.1 12.8 %copy-start.3 = (f32[16,2048]{1,0:T(8,128)S(1)}, f32[16,2048]{1,0:T(8,128)}, u32[]{:S(2)}) copy-start(f32[16,2048]{1,0:T(8,128)} %res.1) | copy-start | bytes 393220
  7.2 39.4 %copy-start.2 = (f32[16,16384]{1,0:T(8,128)S(1)}, f32[16,16384]{1,0:T(8,128)}, u32[]{:S(2)}) copy-start(f32[16,16384]{1,0:T(8,128)} %model.1) | copy-start | bytes 3145732
  19.9 26.7 %copy-start = (f32[16,16384]{1,0:T(8,128)S(1)}, f32[16,16384]{1,0:T(8,128)}, u32[]{:S(2)}) copy-start(f32[16,16384]{1,0:T(8,128)} %dirn.1) | copy-start | bytes 3145732
